TPU v7x, 256 devices: a whole 4x4x8 slice. The times are simulated.
256 devices in a mesh: row: 16 (over z, core), col: 8 (over y_hi, x), rep: 2 (over y_lo).
Axes of the slice: x: 4, y: 4 (y_hi: 2, y_lo: 2; y = y_hi * 2 + y_lo), z: 8, core: 2. Of those that a mesh axis runs over, the one named last changes fastest.
Arguments:
- node_features: bfloat16 [65536, 256], P(('row', 'col', 'rep')), may hold values from -6 to 6
- weight: bfloat16 [256, 256], replicated, may hold values from -0.375 to 0.375
- cotangent: bfloat16 [65536, 256], P(('col', 'rep', 'row')), may hold values from -6 to 6
- adjacency_blocks: bfloat16 [16, 16, 256, 128, 128], P(('col', 'rep'), 'row'), may hold values from -0.0625 to 0.0625
- block_coords: int32 [16, 16, 2, 256], P(('col', 'rep'), 'row'), may hold values from 0 to 31, as said below
- block_counts: int32 [16, 16], P(('col', 'rep'), 'row'), may hold values from 1 to 256, as said below
Outputs:
- hidden: bfloat16 [65536, 256], P(('col', 'rep', 'row'))
- weight_grad: float32 [256, 256], replicated
- feature_grad: bfloat16 [65536, 256], P(('row', 'col', 'rep'))
Inputs may be any that keep to these rules, and one draw needn't show every extreme that they name: block_coords[i, r, 0, k] is a block row below 32 and block_coords[i, r, 1, k] a block column below 32; within a tile the first min(256, 1024) slots name distinct positions. Only the first block_counts[i, r] slots of tile (i, r) belong to the adjacency; the values and coordinates in its other slots are not part of it.
All inputs are finite; a program needn't handle non-finite values.
Results may differ from a plain program's by a relative error of at most 0.029.
Values may be sent and summed in bfloat16 or wider, within the bound.
No kernel may reach another device: no remote copies, remote signals or barrier semaphores. Data moves between devices by JAX's collectives and lax.ppermute only.
A program may use at most 128 MiB of HBM per device.

v0:
```python
import math
import jax
import jax.numpy as jnp
from jax import lax
from jax.sharding import PartitionSpec as P


def silu_slope(values):
    sigma = jax.nn.sigmoid(values)
    return sigma * (1.0 + values * (1.0 - sigma))


def tile_product(blocks, coords, filled, source, out_blocks, flipped):
    slot_total = blocks.shape[0]
    block_size = blocks.shape[1]
    feature_width = source.shape[1]
    group_size = math.gcd(slot_total, 64)
    groups = slot_total // group_size
    source_blocks = source.reshape(-1, block_size, feature_width)
    take_index = coords[0] if flipped else coords[1]
    put_index = coords[1] if flipped else coords[0]
    active = (jnp.arange(slot_total, dtype=jnp.int32) < filled).astype(jnp.float32)
    einsum_form = "kba,kbf->kaf" if flipped else "kab,kbf->kaf"
    targets = jnp.arange(out_blocks, dtype=jnp.int32)

    def accumulate(running, pieces):
        block_group, take_group, put_group, active_group = pieces
        gathered = source_blocks[take_group]
        product = jnp.einsum(einsum_form, block_group, gathered, preferred_element_type=jnp.float32)
        placing = (put_group[:, None] == targets[None, :]).astype(jnp.float32) * active_group[
            :, None
        ]
        flat = product.reshape(group_size, block_size * feature_width)
        placed = lax.dot_general(
            placing,
            flat,
            (((0,), (0,)), ((), ())),
            precision=lax.Precision.HIGHEST,
            preferred_element_type=jnp.float32,
        )
        return (running + placed, None)

    running = jnp.zeros((out_blocks, block_size * feature_width), jnp.float32)
    running, _ = lax.scan(
        accumulate,
        running,
        (
            blocks.reshape(groups, group_size, block_size, block_size),
            take_index.reshape(groups, group_size),
            put_index.reshape(groups, group_size),
            active.reshape(groups, group_size),
        ),
    )
    return running.reshape(out_blocks * block_size, feature_width)


def body(node_features, weight, cotangent, adjacency_blocks, block_coords, block_counts):
    blocks = adjacency_blocks[0, 0]
    coords = block_coords[0, 0]
    filled = block_counts[0, 0]
    block_size = blocks.shape[-1]
    local_nodes = node_features.shape[0]
    row_devices = lax.axis_size("row")
    node_total = local_nodes * row_devices * lax.axis_size("col") * lax.axis_size("rep")
    tile_rows = local_nodes * row_devices
    column_feats = lax.all_gather(node_features, ("col", "rep"), axis=0, tiled=True)
    tile_cols = column_feats.shape[0]
    partial_value = tile_product(
        blocks, coords, filled, column_feats, tile_rows // block_size, False
    )
    own_sum = lax.psum_scatter(
        partial_value.astype(jnp.bfloat16), "row", scatter_dimension=0, tiled=True
    )
    pre_act = jnp.dot(own_sum, weight, preferred_element_type=jnp.float32)
    hidden = jax.nn.silu(pre_act).astype(jnp.bfloat16)
    own_grad = (cotangent.astype(jnp.float32) * silu_slope(pre_act)).astype(jnp.bfloat16)
    own_mixed_grad = jnp.dot(own_grad, weight.T, preferred_element_type=jnp.float32).astype(
        jnp.bfloat16
    )
    panel_grad = lax.all_gather(own_mixed_grad, "row", axis=0, tiled=True)
    weight_part = lax.dot_general(
        own_sum, own_grad, (((0,), (0,)), ((), ())), preferred_element_type=jnp.float32
    )
    weight_grad = lax.psum(weight_part, ("row", "col", "rep")) / math.sqrt(node_total)
    back_terms = tile_product(blocks, coords, filled, panel_grad, tile_cols // block_size, True)
    feature_grad = lax.psum_scatter(
        back_terms.astype(jnp.bfloat16), ("col", "rep"), scatter_dimension=0, tiled=True
    )
    return (hidden, weight_grad, feature_grad)


def solution(mesh):
    in_specs = (
        P(("row", "col", "rep"), None),
        P(),
        P(("col", "rep", "row"), None),
        P(("col", "rep"), "row", None, None, None),
        P(("col", "rep"), "row", None, None),
        P(("col", "rep"), "row"),
    )
    out_specs = (P(("col", "rep", "row"), None), P(), P(("row", "col", "rep"), None))
    return jax.shard_map(body, mesh=mesh, in_specs=in_specs, out_specs=out_specs, check_vma=False)
```

profile of v0, /device:TPU:32, one launch (start us, length us, event | category | flops | bytes accessed | tf_op | source)
XLA Modules:
  0.0 642.4 jit_solution(17018396184696318942)
XLA Ops:
  9.6 81.7 %all-gather.3.cloned.1.call-done = bf16[4096,256]{1,0:T(8,128)(2,1)} async-done(((bf16[256,256]{1,0:T(8,128)(2,1)}), bf16[4096,256]{1,0:T(8,128)(2,1)}) %all-gather.3.cloned.1.call-update) | async-done | bytes 2097168 | tf_op jit(solution)/shard_map/all_gather | solution.py:66
  91.3 99.7 %while.22 = (s32[]{:T(128)}, f32[32,32768]{1,0:T(8,128)}, s32[4,64]{1,0:T(4,128)S(1)}, f32[4,64]{1,0:T(4,128)S(1)}, bf16[4,64,128,128]{3,2,1,0:T(8,128)(2,1)}, /...) while((s32[]{:T(128)}, f32[32,32768]{1,0:T(8,128)}, ...), condition=%wide.region_1.2_spmd.clone, body=%wide.region_0.1_spmd.clone.sunk | while | flops 1344279808 | bytes 56630384 | solution.py:44
  99.7 8.0 %copy.16 = f32[8,8,128,256]{3,1,2,0:T(8,128)} copy(f32[8,8,128,256]{3,2,1,0:T(8,128)S(1)} %bitcast.88) | data formatting | bytes 16777216 | tf_op jit(solution)/shard_map/while
  107.7 8.0 %convolution_add_fusion.4 = f32[32,32768]{1,0:T(8,128)} fusion(f32[64,32768]{1,0:T(8,128)} %bitcast.86, f32[32,32768]{1,0:T(8,128)} %get-tuple-element.276, pred[]{:T(512)S(6)} %compare.6, f32[64]{0:T(128)S(1)} %fusion.64, s32[64]{0:T(128)S(1)} %fusion.65), kind=kOutput, calls=%fused_computation.4.clone.1 | convolution fusion | flops 807407616 | bytes 16777728 | tf_op jit(solution)/shard_map/while/body/eval_jaxpr/dot_general | solution.py:34
  124.1 8.0 %copy.16 = f32[8,8,128,256]{3,1,2,0:T(8,128)} copy(f32[8,8,128,256]{3,2,1,0:T(8,128)S(1)} %bitcast.88) | data formatting | bytes 16777216 | tf_op jit(solution)/shard_map/while
  132.1 8.7 %convolution_add_fusion.4 = f32[32,32768]{1,0:T(8,128)} fusion(f32[64,32768]{1,0:T(8,128)} %bitcast.86, f32[32,32768]{1,0:T(8,128)} %get-tuple-element.276, pred[]{:T(512)S(6)} %compare.6, f32[64]{0:T(128)S(1)} %fusion.64, s32[64]{0:T(128)S(1)} %fusion.65), kind=kOutput, calls=%fused_computation.4.clone.1 | convolution fusion | flops 807407616 | bytes 16777728 | tf_op jit(solution)/shard_map/while/body/eval_jaxpr/dot_general | solution.py:34
  149.2 8.0 %copy.16 = f32[8,8,128,256]{3,1,2,0:T(8,128)} copy(f32[8,8,128,256]{3,2,1,0:T(8,128)S(1)} %bitcast.88) | data formatting | bytes 16777216 | tf_op jit(solution)/shard_map/while
  157.2 8.7 %convolution_add_fusion.4 = f32[32,32768]{1,0:T(8,128)} fusion(f32[64,32768]{1,0:T(8,128)} %bitcast.86, f32[32,32768]{1,0:T(8,128)} %get-tuple-element.276, pred[]{:T(512)S(6)} %compare.6, f32[64]{0:T(128)S(1)} %fusion.64, s32[64]{0:T(128)S(1)} %fusion.65), kind=kOutput, calls=%fused_computation.4.clone.1 | convolution fusion | flops 807407616 | bytes 16777728 | tf_op jit(solution)/shard_map/while/body/eval_jaxpr/dot_general | solution.py:34
  174.3 8.0 %copy.16 = f32[8,8,128,256]{3,1,2,0:T(8,128)} copy(f32[8,8,128,256]{3,2,1,0:T(8,128)S(1)} %bitcast.88) | data formatting | bytes 16777216 | tf_op jit(solution)/shard_map/while
  182.3 8.7 %convolution_add_fusion.4 = f32[32,32768]{1,0:T(8,128)} fusion(f32[64,32768]{1,0:T(8,128)} %bitcast.86, f32[32,32768]{1,0:T(8,128)} %get-tuple-element.276, pred[]{:T(512)S(6)} %compare.6, f32[64]{0:T(128)S(1)} %fusion.64, s32[64]{0:T(128)S(1)} %fusion.65), kind=kOutput, calls=%fused_computation.4.clone.1 | convolution fusion | flops 807407616 | bytes 16777728 | tf_op jit(solution)/shard_map/while/body/eval_jaxpr/dot_general | solution.py:34
  195.8 56.5 %reduce-scatter.3.cloned.1.call-done = bf16[256,256]{1,0:T(8,128)(2,1)} async-done(((bf16[4096,256]{1,0:T(8,128)(2,1)}), bf16[256,256]{1,0:T(8,128)(2,1)}) %reduce-scatter.3.cloned.1.call-update) | async-done | bytes 131088 | tf_op jit(solution)/shard_map/reduce_scatter | solution.py:71
  255.1 12.0 %copy.9 = bf16[1,1,256,128,128]{3,4,2,1,0:T(8,128)(2,1)} copy(bf16[1,1,256,128,128]{4,3,2,1,0:T(8,128)(2,1)} %bitcast.93) | data formatting | bytes 16777216 | tf_op args[3]
  268.3 27.7 %all-gather.5.cloned.1.call-done = bf16[4096,256]{1,0:T(8,128)(2,1)} async-done(((bf16[256,256]{1,0:T(8,128)(2,1)}), bf16[4096,256]{1,0:T(8,128)(2,1)}) %all-gather.5.cloned.1.call-update) | async-done | bytes 2097168 | tf_op jit(solution)/shard_map/all_gather | solution.py:80
  296.0 99.8 %while.23 = (s32[]{:T(128)}, f32[32,32768]{1,0:T(8,128)}, s32[4,64]{1,0:T(4,128)S(1)}, f32[4,64]{1,0:T(4,128)S(1)}, bf16[4,64,128,128]{2,3,1,0:T(8,128)(2,1)}, /...) while((s32[]{:T(128)}, f32[32,32768]{1,0:T(8,128)}, ...), condition=%wide.region_5.6_spmd.clone, body=%wide.region_4.5_spmd.clone.sunk | while | flops 1344279808 | bytes 56630384 | solution.py:44
  304.5 8.0 %copy.17 = f32[8,8,128,256]{3,1,2,0:T(8,128)} copy(f32[8,8,128,256]{3,2,1,0:T(8,128)S(1)} %bitcast.89) | data formatting | bytes 16777216 | tf_op jit(solution)/shard_map/while
  312.4 8.0 %convolution_add_fusion.5 = f32[32,32768]{1,0:T(8,128)} fusion(f32[64,32768]{1,0:T(8,128)} %bitcast.87, f32[32,32768]{1,0:T(8,128)} %get-tuple-element.303, pred[]{:T(512)S(6)} %compare.7, f32[64]{0:T(128)S(1)} %fusion.72, s32[64]{0:T(128)S(1)} %fusion.73), kind=kOutput, calls=%fused_computation.24.clone.1 | convolution fusion | flops 807407616 | bytes 16777728 | tf_op jit(solution)/shard_map/while/body/eval_jaxpr/dot_general | solution.py:34
  328.9 8.0 %copy.17 = f32[8,8,128,256]{3,1,2,0:T(8,128)} copy(f32[8,8,128,256]{3,2,1,0:T(8,128)S(1)} %bitcast.89) | data formatting | bytes 16777216 | tf_op jit(solution)/shard_map/while
  336.9 8.7 %convolution_add_fusion.5 = f32[32,32768]{1,0:T(8,128)} fusion(f32[64,32768]{1,0:T(8,128)} %bitcast.87, f32[32,32768]{1,0:T(8,128)} %get-tuple-element.303, pred[]{:T(512)S(6)} %compare.7, f32[64]{0:T(128)S(1)} %fusion.72, s32[64]{0:T(128)S(1)} %fusion.73), kind=kOutput, calls=%fused_computation.24.clone.1 | convolution fusion | flops 807407616 | bytes 16777728 | tf_op jit(solution)/shard_map/while/body/eval_jaxpr/dot_general | solution.py:34
  354.1 8.0 %copy.17 = f32[8,8,128,256]{3,1,2,0:T(8,128)} copy(f32[8,8,128,256]{3,2,1,0:T(8,128)S(1)} %bitcast.89) | data formatting | bytes 16777216 | tf_op jit(solution)/shard_map/while
  362.0 8.6 %convolution_add_fusion.5 = f32[32,32768]{1,0:T(8,128)} fusion(f32[64,32768]{1,0:T(8,128)} %bitcast.87, f32[32,32768]{1,0:T(8,128)} %get-tuple-element.303, pred[]{:T(512)S(6)} %compare.7, f32[64]{0:T(128)S(1)} %fusion.72, s32[64]{0:T(128)S(1)} %fusion.73), kind=kOutput, calls=%fused_computation.24.clone.1 | convolution fusion | flops 807407616 | bytes 16777728 | tf_op jit(solution)/shard_map/while/body/eval_jaxpr/dot_general | solution.py:34
  379.2 8.0 %copy.17 = f32[8,8,128,256]{3,1,2,0:T(8,128)} copy(f32[8,8,128,256]{3,2,1,0:T(8,128)S(1)} %bitcast.89) | data formatting | bytes 16777216 | tf_op jit(solution)/shard_map/while
  387.1 8.7 %convolution_add_fusion.5 = f32[32,32768]{1,0:T(8,128)} fusion(f32[64,32768]{1,0:T(8,128)} %bitcast.87, f32[32,32768]{1,0:T(8,128)} %get-tuple-element.303, pred[]{:T(512)S(6)} %compare.7, f32[64]{0:T(128)S(1)} %fusion.72, s32[64]{0:T(128)S(1)} %fusion.73), kind=kOutput, calls=%fused_computation.24.clone.1 | convolution fusion | flops 807407616 | bytes 16777728 | tf_op jit(solution)/shard_map/while/body/eval_jaxpr/dot_general | solution.py:34
  400.6 148.2 %all-reduce.2.cloned.1.call-done = f32[256,256]{1,0:T(8,128)} async-done(((f32[256,256]{1,0:T(8,128)}), f32[256,256]{1,0:T(8,128)}) %all-reduce.2.cloned.1.call-update) | async-done | bytes 262160 | tf_op jit(solution)/shard_map/psum | solution.py:84
  550.5 85.3 %reduce-scatter.5.cloned.1.call-done = bf16[256,256]{1,0:T(8,128)(2,1)} async-done(((bf16[4096,256]{1,0:T(8,128)(2,1)}), bf16[256,256]{1,0:T(8,128)(2,1)}) %reduce-scatter.5.cloned.1.call-update) | async-done | bytes 131088 | tf_op jit(solution)/shard_map/reduce_scatter | solution.py:86
  (80 shorter events, 84.5 us)
Async XLA Ops:
  7.2 245.1 %copy-start = (bf16[256,256]{1,0:T(8,128)(2,1)S(1)}, bf16[256,256]{1,0:T(8,128)(2,1)}, u32[]{:S(2)}) copy-start(bf16[256,256]{1,0:T(8,128)(2,1)} %param.11) | copy-start | bytes 393220
  7.2 84.1 %all-gather.3.cloned.1.call-start = ((), (), s32[]{:S(2)}) async-start(), calls=%async_computation.2 | async-start | bytes 2228224 | tf_op jit(solution)/shard_map/all_gather | solution.py:66
  7.9 244.4 %reduce-scatter.3.cloned.1.call-start = ((), (), s32[]{:S(2)}) async-start(), calls=%async_computation.3 | async-start | bytes 2228224 | tf_op jit(solution)/shard_map/reduce_scatter | solution.py:71
  193.4 58.9 %copy-start.3 = (bf16[256,256]{1,0:T(8,128)(2,1)S(1)}, bf16[256,256]{1,0:T(8,128)(2,1)}, u32[]{:S(2)}) copy-start(bf16[256,256]{1,0:T(8,128)(2,1)} %param.12) | copy-start | bytes 393220
  195.8 100.3 %all-gather.5.cloned.1.call-start = ((), (), s32[]{:S(2)}) async-start(), calls=%async_computation.5 | async-start | bytes 2228224 | tf_op jit(solution)/shard_map/all_gather | solution.py:80
  255.0 12.1 %copy-start.2 = (bf16[256,256]{1,0:T(8,128)(2,1)S(1)}, bf16[256,256]{1,0:T(8,128)(2,1)}, u32[]{:S(2)}) copy-start(bf16[256,256]{1,0:T(8,128)(2,1)} %reduce-scatter.3.cloned.1.call-done) | copy-start | bytes 393220
  255.0 293.8 %all-reduce.2.cloned.1.call-start = ((), (), s32[]{:S(2)}) async-start(), calls=%async_computation.4 | async-start | bytes 524288 | tf_op jit(solution)/shard_map/psum | solution.py:84
  268.1 367.8 %reduce-scatter.5.cloned.1.call-start = ((), (), s32[]{:S(2)}) async-start(), calls=%async_computation.6 | async-start | bytes 2228224 | tf_op jit(solution)/shard_map/reduce_scatter | solution.py:86
  395.8 240.0 %copy-start.1 = (bf16[256,256]{1,0:T(8,128)(2,1)S(1)}, bf16[256,256]{1,0:T(8,128)(2,1)}, u32[]{:S(2)}) copy-start(bf16[256,256]{1,0:T(8,128)(2,1)} %param.11) | copy-start | bytes 393220
Sparse Core Ops, SparseCore 0:
  9.8 81.4 all-gather.2
  195.9 56.3 reduce-scatter.2
  255.2 40.8 all-gather.4
  301.9 246.9 all-reduce.1
  551.8 83.9 reduce-scatter.4
where the time goes:
time: 643 us; the launch traced here: 642 us
  waiting for transfers between devices  400 us (62%)
  local copies, waits for them, and re-layouts  116 us (18%)
  matrix products  104 us (16%)
  between operations  14.5 us (2%)
  other arithmetic  6.61 us (1%)
    psum x1, waiting for transfers between devices, body(): lax.psum(weight_part, ('row', 'col', 'rep')) / math.sqrt(node_total)  148 us
    reduce_scatter x1, waiting for transfers between devices, body(): lax.psum_scatter(back_terms.astype(jnp.bfloat16), ('col', 'rep'), scatter...  85.3 us
    all_gather x1, waiting for transfers between devices, body(): lax.all_gather(node_features, ('col', 'rep'), axis=0, tiled=True)  81.7 us
    dot_general x8, matrix products, accumulate(): lax.dot_general(placing, flat, (((0,), (0,)), ((), ())), precision=lax.Pr...  68 us
    while x8, local copies, waits for them, and re-layouts  63.7 us
    reduce_scatter x1, waiting for transfers between devices, body(): lax.psum_scatter(partial_value.astype(jnp.bfloat16), 'row', scatter_dimen...  56.5 us
    gather x8, local copies, waits for them, and re-layouts, accumulate(): gathered = source_blocks[take_group]  34.8 us
    dot_general x8, matrix products, accumulate(): jnp.einsum(einsum_form, block_group, gathered, preferred_element_type=jnp...  32.6 us
  transfers between devices with their start and end apart: 5, of which 5 were waited for; matrix products, arithmetic and copies ran while one was open for 19% of the time, Pallas kernels for 0%

commit v1 on v0

--- a/solution.py
+++ b/solution.py
@@ -77,7 +77,27 @@
     own_mixed_grad = jnp.dot(own_grad, weight.T, preferred_element_type=jnp.float32).astype(
         jnp.bfloat16
     )
-    panel_grad = lax.all_gather(own_mixed_grad, "row", axis=0, tiled=True)
+    count, position, rows = (lax.axis_size("row"), lax.axis_index("row"), own_mixed_grad.shape[0])
+    right = [(i, (i + 1) % count) for i in range(count)]
+    left = [(i, (i - 1) % count) for i in range(count)]
+    out = jnp.zeros(
+        (*own_mixed_grad.shape[:0], count * rows, *own_mixed_grad.shape[0 + 1 :]),
+        own_mixed_grad.dtype,
+    )
+    out = lax.dynamic_update_slice_in_dim(out, own_mixed_grad, position * rows, axis=0)
+    from_left = from_right = own_mixed_grad
+    halfway = count // 2
+    for turn in range(1, halfway + 1):
+        from_left = lax.ppermute(from_left, "row", right)
+        out = lax.dynamic_update_slice_in_dim(
+            out, from_left, (position - turn) % count * rows, axis=0
+        )
+        if turn < count - halfway:
+            from_right = lax.ppermute(from_right, "row", left)
+            out = lax.dynamic_update_slice_in_dim(
+                out, from_right, (position + turn) % count * rows, axis=0
+            )
+    panel_grad = out
     weight_part = lax.dot_general(
         own_sum, own_grad, (((0,), (0,)), ((), ())), preferred_element_type=jnp.float32
     )

time: 643 us -> 603 us (0.938)
  waiting for transfers between devices: 400 us -> 349 us
  starting transfers between devices: 0.38 us -> 17.6 us
    psum x1, waiting for transfers between devices: 148 us -> 115 us  [body(): lax.psum(weight_part, ('row', 'col', 'rep')) / math.sqrt(node_total)]
    all_gather x1 -> x0, waiting for transfers between devices: 27.7 us -> none  [body(): panel_grad = lax.all_gather(own_mixed_grad, 'row', axis=0, tiled=True)]
    ppermute x0 -> x15, waiting for transfers between devices: none -> 22.2 us  [the longest x8 22.1 us: body(): from_left = lax.ppermute(from_left, 'row', right)]
    ppermute x0 -> x15, starting transfers between devices: none -> 17.3 us  [the longest x7 17.3 us: body(): from_right = lax.ppermute(from_right, 'row', left)]
    reduce_scatter x1, waiting for transfers between devices: 56.5 us -> 44.3 us  [body(): lax.psum_scatter(partial_value.astype(jnp.bfloat16), 'row', scatter_dimen...]
  transfers between devices with their start and end apart: 5 -> 19, of which waited for: 5 -> 12; matrix products, arithmetic and copies ran while one was open for 19% -> 19% of each run, Pallas kernels for 0% -> 0%
where the time goes in v1:
time: 603 us; the launch traced here: 602 us
  waiting for transfers between devices  349 us (58%)
  local copies, waits for them, and re-layouts  110 us (18%)
  matrix products  104 us (17%)
  starting transfers between devices  17.6 us (3%)
  between operations  14.9 us (2%)
  other arithmetic  6.58 us (1%)
    psum x1, waiting for transfers between devices, body(): lax.psum(weight_part, ('row', 'col', 'rep')) / math.sqrt(node_total)  115 us
    reduce_scatter x1, waiting for transfers between devices, body(): lax.psum_scatter(back_terms.astype(jnp.bfloat16), ('col', 'rep'), scatter...  85.3 us
    all_gather x1, waiting for transfers between devices, body(): lax.all_gather(node_features, ('col', 'rep'), axis=0, tiled=True)  81.7 us
    dot_general x8, matrix products, accumulate(): lax.dot_general(placing, flat, (((0,), (0,)), ((), ())), precision=lax.Pr...  68.1 us
    while x8, local copies, waits for them, and re-layouts  63.8 us
    reduce_scatter x1, waiting for transfers between devices, body(): lax.psum_scatter(partial_value.astype(jnp.bfloat16), 'row', scatter_dimen...  44.3 us
    dot_general x8, matrix products, accumulate(): jnp.einsum(einsum_form, block_group, gathered, preferred_element_type=jnp...  32.5 us
    gather x8, local copies, waits for them, and re-layouts, accumulate(): gathered = source_blocks[take_group]  28.5 us
  transfers between devices with their start and end apart: 19, of which 12 were waited for; matrix products, arithmetic and copies ran while one was open for 19% of the time, Pallas kernels for 0%

profile of v1, /device:TPU:32, one launch (start us, length us, event | category | flops | bytes accessed | tf_op | source)
XLA Modules:
  0.0 602.3 jit_solution(9687051765063613450)
XLA Ops:
  9.6 81.7 %all-gather.2.cloned.1.call-done = bf16[4096,256]{1,0:T(8,128)(2,1)} async-done(((bf16[256,256]{1,0:T(8,128)(2,1)}), bf16[4096,256]{1,0:T(8,128)(2,1)}) %all-gather.2.cloned.1.call-update) | async-done | bytes 2097168 | tf_op jit(solution)/shard_map/all_gather | solution.py:66
  91.3 99.8 %while.22 = (s32[]{:T(128)}, f32[32,32768]{1,0:T(8,128)}, s32[4,64]{1,0:T(4,128)S(1)}, f32[4,64]{1,0:T(4,128)S(1)}, bf16[4,64,128,128]{3,2,1,0:T(8,128)(2,1)}, /...) while((s32[]{:T(128)}, f32[32,32768]{1,0:T(8,128)}, ...), condition=%wide.region_1.2_spmd.clone, body=%wide.region_0.1_spmd.clone.sunk | while | flops 1344279808 | bytes 56630384 | solution.py:44
  99.7 8.0 %copy.16 = f32[8,8,128,256]{3,1,2,0:T(8,128)} copy(f32[8,8,128,256]{3,2,1,0:T(8,128)S(1)} %bitcast.88) | data formatting | bytes 16777216 | tf_op jit(solution)/shard_map/while
  107.7 8.0 %convolution_add_fusion.4 = f32[32,32768]{1,0:T(8,128)} fusion(f32[64,32768]{1,0:T(8,128)} %bitcast.86, f32[32,32768]{1,0:T(8,128)} %get-tuple-element.278, pred[]{:T(512)S(6)} %compare.21, f32[64]{0:T(128)S(1)} %fusion.64, s32[64]{0:T(128)S(1)} %fusion.65), kind=kOutput, calls=%fused_computation.4.clone.1 | convolution fusion | flops 807407616 | bytes 16777728 | tf_op jit(solution)/shard_map/while/body/eval_jaxpr/dot_general | solution.py:34
  124.2 8.0 %copy.16 = f32[8,8,128,256]{3,1,2,0:T(8,128)} copy(f32[8,8,128,256]{3,2,1,0:T(8,128)S(1)} %bitcast.88) | data formatting | bytes 16777216 | tf_op jit(solution)/shard_map/while
  132.2 8.7 %convolution_add_fusion.4 = f32[32,32768]{1,0:T(8,128)} fusion(f32[64,32768]{1,0:T(8,128)} %bitcast.86, f32[32,32768]{1,0:T(8,128)} %get-tuple-element.278, pred[]{:T(512)S(6)} %compare.21, f32[64]{0:T(128)S(1)} %fusion.64, s32[64]{0:T(128)S(1)} %fusion.65), kind=kOutput, calls=%fused_computation.4.clone.1 | convolution fusion | flops 807407616 | bytes 16777728 | tf_op jit(solution)/shard_map/while/body/eval_jaxpr/dot_general | solution.py:34
  149.3 8.0 %copy.16 = f32[8,8,128,256]{3,1,2,0:T(8,128)} copy(f32[8,8,128,256]{3,2,1,0:T(8,128)S(1)} %bitcast.88) | data formatting | bytes 16777216 | tf_op jit(solution)/shard_map/while
  157.3 8.7 %convolution_add_fusion.4 = f32[32,32768]{1,0:T(8,128)} fusion(f32[64,32768]{1,0:T(8,128)} %bitcast.86, f32[32,32768]{1,0:T(8,128)} %get-tuple-element.278, pred[]{:T(512)S(6)} %compare.21, f32[64]{0:T(128)S(1)} %fusion.64, s32[64]{0:T(128)S(1)} %fusion.65), kind=kOutput, calls=%fused_computation.4.clone.1 | convolution fusion | flops 807407616 | bytes 16777728 | tf_op jit(solution)/shard_map/while/body/eval_jaxpr/dot_general | solution.py:34
  174.4 8.0 %copy.16 = f32[8,8,128,256]{3,1,2,0:T(8,128)} copy(f32[8,8,128,256]{3,2,1,0:T(8,128)S(1)} %bitcast.88) | data formatting | bytes 16777216 | tf_op jit(solution)/shard_map/while
  182.4 8.7 %convolution_add_fusion.4 = f32[32,32768]{1,0:T(8,128)} fusion(f32[64,32768]{1,0:T(8,128)} %bitcast.86, f32[32,32768]{1,0:T(8,128)} %get-tuple-element.278, pred[]{:T(512)S(6)} %compare.21, f32[64]{0:T(128)S(1)} %fusion.64, s32[64]{0:T(128)S(1)} %fusion.65), kind=kOutput, calls=%fused_computation.4.clone.1 | convolution fusion | flops 807407616 | bytes 16777728 | tf_op jit(solution)/shard_map/while/body/eval_jaxpr/dot_general | solution.py:34
  196.2 12.0 %copy.9 = bf16[1,1,256,128,128]{3,4,2,1,0:T(8,128)(2,1)} copy(bf16[1,1,256,128,128]{4,3,2,1,0:T(8,128)(2,1)} %bitcast.93) | data formatting | bytes 16777216 | tf_op args[3]
  208.2 44.3 %reduce-scatter.3.cloned.1.call-done = bf16[256,256]{1,0:T(8,128)(2,1)} async-done(((bf16[4096,256]{1,0:T(8,128)(2,1)}), bf16[256,256]{1,0:T(8,128)(2,1)}) %reduce-scatter.3.cloned.1.call-update) | async-done | bytes 131088 | tf_op jit(solution)/shard_map/reduce_scatter | solution.py:71
  290.3 5.6 collective-permute-done.14
  295.9 93.5 %while.23 = (s32[]{:T(128)}, f32[32,32768]{1,0:T(8,128)}, s32[4,64]{1,0:T(4,128)S(1)}, f32[4,64]{1,0:T(4,128)S(1)}, bf16[4,64,128,128]{2,3,1,0:T(8,128)(2,1)}, /...) while((s32[]{:T(128)}, f32[32,32768]{1,0:T(8,128)}, ...), condition=%wide.region_5.6_spmd.clone, body=%wide.region_4.5_spmd.clone.sunk | while | flops 1344279808 | bytes 56630384 | solution.py:44
  302.8 8.0 %copy.17 = f32[8,8,128,256]{3,1,2,0:T(8,128)} copy(f32[8,8,128,256]{3,2,1,0:T(8,128)S(1)} %bitcast.89) | data formatting | bytes 16777216 | tf_op jit(solution)/shard_map/while
  310.7 8.0 %convolution_add_fusion.5 = f32[32,32768]{1,0:T(8,128)} fusion(f32[64,32768]{1,0:T(8,128)} %bitcast.87, f32[32,32768]{1,0:T(8,128)} %get-tuple-element.305, pred[]{:T(512)S(6)} %compare.22, f32[64]{0:T(128)S(1)} %fusion.72, s32[64]{0:T(128)S(1)} %fusion.73), kind=kOutput, calls=%fused_computation.24.clone.1 | convolution fusion | flops 807407616 | bytes 16777728 | tf_op jit(solution)/shard_map/while/body/eval_jaxpr/dot_general | solution.py:34
  325.6 8.0 %copy.17 = f32[8,8,128,256]{3,1,2,0:T(8,128)} copy(f32[8,8,128,256]{3,2,1,0:T(8,128)S(1)} %bitcast.89) | data formatting | bytes 16777216 | tf_op jit(solution)/shard_map/while
  333.6 8.7 %convolution_add_fusion.5 = f32[32,32768]{1,0:T(8,128)} fusion(f32[64,32768]{1,0:T(8,128)} %bitcast.87, f32[32,32768]{1,0:T(8,128)} %get-tuple-element.305, pred[]{:T(512)S(6)} %compare.22, f32[64]{0:T(128)S(1)} %fusion.72, s32[64]{0:T(128)S(1)} %fusion.73), kind=kOutput, calls=%fused_computation.24.clone.1 | convolution fusion | flops 807407616 | bytes 16777728 | tf_op jit(solution)/shard_map/while/body/eval_jaxpr/dot_general | solution.py:34
  349.2 8.0 %copy.17 = f32[8,8,128,256]{3,1,2,0:T(8,128)} copy(f32[8,8,128,256]{3,2,1,0:T(8,128)S(1)} %bitcast.89) | data formatting | bytes 16777216 | tf_op jit(solution)/shard_map/while
  357.2 8.7 %convolution_add_fusion.5 = f32[32,32768]{1,0:T(8,128)} fusion(f32[64,32768]{1,0:T(8,128)} %bitcast.87, f32[32,32768]{1,0:T(8,128)} %get-tuple-element.305, pred[]{:T(512)S(6)} %compare.22, f32[64]{0:T(128)S(1)} %fusion.72, s32[64]{0:T(128)S(1)} %fusion.73), kind=kOutput, calls=%fused_computation.24.clone.1 | convolution fusion | flops 807407616 | bytes 16777728 | tf_op jit(solution)/shard_map/while/body/eval_jaxpr/dot_general | solution.py:34
  372.7 8.0 %copy.17 = f32[8,8,128,256]{3,1,2,0:T(8,128)} copy(f32[8,8,128,256]{3,2,1,0:T(8,128)S(1)} %bitcast.89) | data formatting | bytes 16777216 | tf_op jit(solution)/shard_map/while
  380.7 8.7 %convolution_add_fusion.5 = f32[32,32768]{1,0:T(8,128)} fusion(f32[64,32768]{1,0:T(8,128)} %bitcast.87, f32[32,32768]{1,0:T(8,128)} %get-tuple-element.305, pred[]{:T(512)S(6)} %compare.22, f32[64]{0:T(128)S(1)} %fusion.72, s32[64]{0:T(128)S(1)} %fusion.73), kind=kOutput, calls=%fused_computation.24.clone.1 | convolution fusion | flops 807407616 | bytes 16777728 | tf_op jit(solution)/shard_map/while/body/eval_jaxpr/dot_general | solution.py:34
  394.2 114.6 %all-reduce.2.cloned.1.call-done = f32[256,256]{1,0:T(8,128)} async-done(((f32[256,256]{1,0:T(8,128)}), f32[256,256]{1,0:T(8,128)}) %all-reduce.2.cloned.1.call-update) | async-done | bytes 262160 | tf_op jit(solution)/shard_map/psum | solution.py:104
  510.5 85.3 %reduce-scatter.5.cloned.1.call-done = bf16[256,256]{1,0:T(8,128)(2,1)} async-done(((bf16[4096,256]{1,0:T(8,128)(2,1)}), bf16[256,256]{1,0:T(8,128)(2,1)}) %reduce-scatter.5.cloned.1.call-update) | async-done | bytes 131088 | tf_op jit(solution)/shard_map/reduce_scatter | solution.py:106
  (123 shorter events, 111.8 us)
Async XLA Ops:
  7.2 245.4 %copy-start = (bf16[256,256]{1,0:T(8,128)(2,1)S(1)}, bf16[256,256]{1,0:T(8,128)(2,1)}, u32[]{:S(2)}) copy-start(bf16[256,256]{1,0:T(8,128)(2,1)} %param.11) | copy-start | bytes 393220
  7.2 84.1 %all-gather.2.cloned.1.call-start = ((), (), s32[]{:S(2)}) async-start(), calls=%async_computation.2 | async-start | bytes 2228224 | tf_op jit(solution)/shard_map/all_gather | solution.py:66
  7.9 244.7 %reduce-scatter.3.cloned.1.call-start = ((), (), s32[]{:S(2)}) async-start(), calls=%async_computation.3 | async-start | bytes 2228224 | tf_op jit(solution)/shard_map/reduce_scatter | solution.py:71
  195.9 312.9 %all-reduce.2.cloned.1.call-start = ((), (), s32[]{:S(2)}) async-start(), calls=%async_computation.4 | async-start | bytes 524288 | tf_op jit(solution)/shard_map/psum | solution.py:104
  196.2 56.4 %copy-start.3 = (bf16[256,256]{1,0:T(8,128)(2,1)S(1)}, bf16[256,256]{1,0:T(8,128)(2,1)}, u32[]{:S(2)}) copy-start(bf16[256,256]{1,0:T(8,128)(2,1)} %param.12) | copy-start | bytes 393220
  252.6 4.1 copy-start.2
  254.9 4.4 collective-permute-start
  254.9 4.4 collective-permute-start.1
  257.6 338.2 %reduce-scatter.5.cloned.1.call-start = ((), (), s32[]{:S(2)}) async-start(), calls=%async_computation.5 | async-start | bytes 2228224 | tf_op jit(solution)/shard_map/reduce_scatter | solution.py:106
  259.3 4.4 collective-permute-start.2
  259.3 4.4 collective-permute-start.3
  263.7 4.4 collective-permute-start.4
  263.7 4.4 collective-permute-start.5
  268.1 5.3 collective-permute-start.6
  268.1 5.3 collective-permute-start.7
  273.4 5.6 collective-permute-start.8
  273.4 5.6 collective-permute-start.9
  279.0 5.6 collective-permute-start.10
  279.0 5.6 collective-permute-start.11
  284.6 5.6 collective-permute-start.12
  284.6 5.6 collective-permute-start.13
  290.2 5.6 collective-permute-start.14
  391.8 204.0 %copy-start.1 = (bf16[256,256]{1,0:T(8,128)(2,1)S(1)}, bf16[256,256]{1,0:T(8,128)(2,1)}, u32[]{:S(2)}) copy-start(bf16[256,256]{1,0:T(8,128)(2,1)} %param.11) | copy-start | bytes 393220
Sparse Core Ops, SparseCore 0:
  9.8 81.4 all-gather.1
  196.0 56.5 reduce-scatter.2
  258.6 250.1 all-reduce.1
  511.8 83.9 reduce-scatter.4
